TPU v7x, 32 devices: a whole 2x2x4 slice. The times are simulated.
32 devices in a mesh: pix: 4 (over y, x), act: 8 (over z, core).
Axes of the slice: x: 2, y: 2, z: 4, core: 2. Of those that a mesh axis runs over, the one named last changes fastest.
Arguments:
- jacobian: bfloat16 [1024, 18432], P('pix', 'act'), may hold values from -0.1875 to 0.1875
- dark_field: float32 [1024], P('pix'), may hold values from -6 to 6
- update: float32 [18432], P('act'), may hold values from -3 to 3
- pixel_mask: int32 [1024], P('pix'), may hold values 0 or 1
- act_mask: int32 [18432], P('act'), may hold values 0 or 1
Outputs:
- gram_matrix: float32 [18432, 18432], P('act', 'pix')
- projected: float32 [18432], P('act')
- predicted: float32 [1024], P('pix')
All inputs are finite; a program needn't handle non-finite values. No bound on the sum of `pixel_mask` or of `act_mask` on one device may be relied on, other than what follows from the above.
Results may differ from a plain program's by a relative error of at most 0.0003.
Values may be sent and summed in bfloat16 or wider, within the bound.
A program may use at most 128 MiB of HBM per device.

v0:
```python
import jax
import jax.numpy as jnp
from jax import lax
from jax.sharding import PartitionSpec as P


def local(jacobian, dark_field, update, pixel_mask, act_mask):
    keep = pixel_mask[:, None] * act_mask[None, :] > 0
    masked_jac = jnp.where(keep, jacobian, jnp.zeros_like(jacobian))
    weighted = pixel_mask.astype(jnp.float32) * dark_field
    strokes = act_mask.astype(jnp.float32) * update
    field_term = jnp.dot(
        weighted, masked_jac, precision=lax.Precision.HIGHEST, preferred_element_type=jnp.float32
    )
    stroke_term = jnp.dot(
        masked_jac, strokes, precision=lax.Precision.HIGHEST, preferred_element_type=jnp.float32
    )
    projected = lax.psum(field_term, "pix")
    predicted = lax.psum(stroke_term, "act")
    full_rows = lax.all_gather(masked_jac, "act", axis=1, tiled=True)
    slice_columns = lax.all_to_all(full_rows, "pix", split_axis=1, concat_axis=0, tiled=True)
    gram_matrix = lax.dot_general(
        lax.all_gather(masked_jac, "pix", axis=0, tiled=True),
        slice_columns,
        (((0,), (0,)), ((), ())),
        preferred_element_type=jnp.float32,
    )
    return (gram_matrix, projected, predicted)


def solution(mesh):
    return jax.shard_map(
        local,
        mesh=mesh,
        in_specs=(P("pix", "act"), P("pix"), P("act"), P("pix"), P("act")),
        out_specs=(P("act", "pix"), P("act"), P("pix")),
        check_vma=False,
    )
```

profile of v0, /device:TPU:5, one launch (start us, length us, event | category | flops | bytes accessed | tf_op | source)
XLA Modules:
  0.0 310.2 jit_solution(17335226479959252770)
XLA Ops:
  8.0 0.0 copy-start.1
  8.0 0.0 copy-start.3
  8.0 0.0 all-gather.5.cloned.1.call-start
  8.1 1.6 copy.8
  9.6 0.0 copy-done.1
  9.7 0.0 copy-done.3
  9.7 1.9 fusion
  11.6 0.0 all-gather.5.cloned.1.call-update
  11.6 92.5 %all-gather.5.cloned.1.call-done = bf16[256,18432]{0,1:T(8,128)(2,1)} async-done(((bf16[256,2304]{0,1:T(8,128)(2,1)}), bf16[256,18432]{0,1:T(8,128)(2,1)}) %all-gather.5.cloned.1.call-update) | async-done | bytes 9437200 | tf_op jit(solution)/shard_map/all_gather | solution.py:20
  104.1 0.0 copy-start.2
  104.1 0.0 copy-start
  104.1 6.1 %all-to-all-start = ((bf16[256,4,4608]{0,2,1:T(8,128)(2,1)}), bf16[256,4,4608]{0,2,1:T(8,128)(2,1)}, u32[]{:S(2)}, u32[]{:S(2)}) async-start(bf16[256,4,4608]{0,2,1:T(8,128)(2,1)} %bitcast.11), calls=%async_computation | async-start | bytes 18874368 | tf_op jit(solution)/shard_map/all_to_all | solution.py:21
  110.3 0.0 copy-start.4
  110.3 0.0 all-gather.3.cloned.1.call-start
  110.3 0.6 all-gather.3.cloned.1.call-update
  110.8 0.0 copy-done.2
  110.9 0.0 copy-done
  110.9 0.5 fusion.2
  111.4 14.1 %psum.15 = f32[256]{0:T(256)} all-reduce(f32[256]{0:T(256)S(1)} %bitcast.13), channel_id=1, replica_groups=mesh['pix'=4,'act'=8] {'act'}, use_global_device_ids=true, to_apply=%region_1.2 | all-reduce | flops 256 | bytes 2048 | tf_op jit(solution)/shard_map/psum | solution.py:19
  125.5 0.0 copy-done.4
  125.5 1.1 convolution_reduce_fusion
  126.6 132.2 %psum.14 = f32[2304]{0:T(1024)} all-reduce(f32[2304]{0:T(1024)S(1)} %convolution_reduce_fusion), channel_id=1, replica_groups=mesh['pix'=4,'act'=8] {'pix'}, use_global_device_ids=true, to_apply=%region_0.1 | all-reduce | flops 2304 | bytes 18432 | tf_op jit(solution)/shard_map/psum | solution.py:18
  258.8 0.0 all-to-all-done
  258.8 12.7 %copy.9 = bf16[4,256,4608]{2,1,0:T(8,128)(2,1)} copy(bf16[4,256,4608]{1,2,0:T(8,128)(2,1)} %bitcast.1) | data formatting | bytes 18874368 | tf_op jit(solution)/shard_map/all_to_all | solution.py:21
  271.5 0.0 all-gather.3.cloned.1.call-done
  271.5 31.2 %fusion.1 = f32[2304,4608]{1,0:T(8,128)} fusion(bf16[1024,2304]{0,1:T(8,128)(2,1)} %all-gather.3.cloned.1.call-done, bf16[1024,4608]{1,0:T(8,128)(2,1)} %bitcast.12), kind=kOutput, calls=%fused_computation.5 | convolution fusion | flops 21743271936 | bytes 56623104 | tf_op jit(solution)/shard_map/dot_general | solution.py:22
  (3 shorter events, 0.0 us)
Async XLA Ops:
  8.0 1.6 copy-start.1
  8.0 1.6 copy-start.3
  8.0 96.1 %all-gather.5.cloned.1.call-start = ((), (), s32[]{:S(2)}) async-start(), calls=%async_computation.2 | async-start | bytes 10616832 | tf_op jit(solution)/shard_map/all_gather | solution.py:20
  104.1 6.7 %copy-start.2 = (f32[2304]{0:T(1024)S(1)}, f32[2304]{0:T(1024)}, u32[]{:S(2)}) copy-start(f32[2304]{0:T(1024)} %param.7) | copy-start | bytes 27652
  104.1 6.7 %copy-start = (bf16[256,2304]{0,1:T(8,128)(2,1)S(1)}, bf16[256,2304]{0,1:T(8,128)(2,1)}, u32[]{:S(2)}) copy-start(bf16[256,2304]{0,1:T(8,128)(2,1)} %fusion) | copy-start | bytes 3538948
  104.1 154.7 %all-to-all-start = ((bf16[256,4,4608]{0,2,1:T(8,128)(2,1)}), bf16[256,4,4608]{0,2,1:T(8,128)(2,1)}, u32[]{:S(2)}, u32[]{:S(2)}) async-start(bf16[256,4,4608]{0,2,1:T(8,128)(2,1)} %bitcast.11), calls=%async_computation | async-start | bytes 18874368 | tf_op jit(solution)/shard_map/all_to_all | solution.py:21
  110.3 15.2 %copy-start.4 = (f32[256]{0:T(256)S(1)}, f32[256]{0:T(256)}, u32[]{:S(2)}) copy-start(f32[256]{0:T(256)} %param.6) | copy-start | bytes 3076
  110.3 161.3 %all-gather.3.cloned.1.call-start = ((), (), s32[]{:S(2)}) async-start(), calls=%async_computation.1 | async-start | bytes 5898240 | tf_op jit(solution)/shard_map/all_gather | solution.py:23
Sparse Core Ops, SparseCore 0:
  11.7 92.3 all-gather.4
Sparse Core Ops, SparseCore 1:
  113.1 131.7 all-gather.2
where the time goes:
time: 315 us; the launch traced here: 310 us
  blocking collectives  146 us (46%)
  waiting for transfers between devices  93.1 us (30%)
  matrix products  32.8 us (10%)
  between operations  15.6 us (5%)
  local copies, waits for them, and re-layouts  14.3 us (5%)
  starting transfers between devices  6.18 us (2%)
    psum x1, blocking collectives, local(): projected = lax.psum(field_term, 'pix')  132 us
    all_gather x1, waiting for transfers between devices, local(): full_rows = lax.all_gather(masked_jac, 'act', axis=1, tiled=True)  92.5 us
    dot_general x1, matrix products, local(): lax.dot_general(lax.all_gather(masked_jac, 'pix', axis=0, tiled=True), sl...  31.2 us
    psum x1, blocking collectives, local(): predicted = lax.psum(stroke_term, 'act')  14.1 us
    all_to_all x1, local copies, waits for them, and re-layouts, local(): lax.all_to_all(full_rows, 'pix', split_axis=1, concat_axis=0, tiled=True)  12.7 us
  transfers between devices with their start and end apart: 3, of which 1 were waited for; matrix products, arithmetic and copies ran while one was open for 5% of the time, Pallas kernels for 0%

commit v1 on v0

v1 whole, which is shorter than its diff:
```python
import functools

import jax
import jax.numpy as jnp
from jax import lax
from jax.experimental import pallas as pl
from jax.experimental.pallas import tpu as pltpu
from jax.sharding import PartitionSpec as P

MESH = pl.DeviceIdType.MESH
F32 = jnp.float32
BF16 = jnp.bfloat16


def mixed(index, step, size):
    bit, out = 1, index
    while bit < size:
        if step & bit:
            out = out + bit - 2 * bit * ((index // bit) % 2)
        bit *= 2
    return out


def gather_kernel(
    npix, ngrp, chunks, via_line, jac, col, row, lhs, rhs, proj, pred,
    mj, relay, terms_f, terms_s, l_recv, r_recv, t_recv, s_recv, f_recv, p_recv, sends, local_sem,
):
    rows, cols = jac.shape
    ch = rows // chunks
    p = lax.axis_index("pix")
    a = lax.axis_index("act")
    z = a // 2
    c = a % 2
    root = p == z
    here = z >= 0
    nact = 2 * ngrp

    barrier = pltpu.get_barrier_semaphore()
    for d in range(1, npix):
        pl.semaphore_signal(barrier, inc=1, device_id={"pix": mixed(p, d, npix), "act": a}, device_id_type=MESH)
    for d in range(1, nact):
        pl.semaphore_signal(barrier, inc=1, device_id={"pix": p, "act": lax.rem(a + d, nact)}, device_id_type=MESH)

    def mask_step(i, carry):
        at = pl.ds(pl.multiple_of(i * 128, 128), 128)
        keep = col[:, 0:1] * row[0:1, at] > 0
        mj[:, at] = jnp.where(keep, jac[:, at].astype(F32), 0.0).astype(BF16)
        return carry

    lax.fori_loop(0, cols // 128, mask_step, 0)
    pl.semaphore_wait(barrier, npix - 1 + nact - 1)

    pending = []

    def send(cond, src, dst, rsem, pix, act):
        ssem = sends.at[len(pending)]

        def make():
            return pltpu.make_async_remote_copy(
                src_ref=src, dst_ref=dst, send_sem=ssem, recv_sem=rsem,
                device_id={"pix": pix, "act": act}, device_id_type=MESH,
            )

        @pl.when(cond)
        def _():
            make().start()

        pending.append((cond, make))

    def arrived(ref, sem):
        pltpu.make_async_copy(ref, ref, sem).wait()

    def at_rows(q, k):
        return pl.ds(pl.multiple_of(q * rows + k * ch, ch), ch)

    my_half = pl.ds(pl.multiple_of(c * cols, 128), cols)
    other_half = pl.ds(pl.multiple_of((1 - c) * cols, 128), cols)

    def l_ref(q, k):
        return lhs.at[at_rows(q, k), :]

    def r_ref(q, k):
        return rhs.at[at_rows(q, k), my_half]

    def own(k):
        return mj.at[pl.ds(k * ch, ch), :]

    up = z + 1 < ngrp
    down = z > 0

    def along_line(cond, src, q, k):
        send(cond & up & (z >= p), src, r_ref(q, k), r_recv.at[q, k], p, a + 2)
        send(cond & down & (z <= p), src, r_ref(q, k), r_recv.at[q, k], p, a - 2)

    def to_twin(cond, src, q, k):
        send(cond, src, r_ref(q, k), t_recv.at[q, k], p, 2 * z + 1 - c)

    for k in range(chunks):
        along_line(root, own(k), p, k)
        if k < via_line:
            send(jnp.logical_not(root) & up, own(k), relay.at[z, k], s_recv.at[z, k], p, a + 2)
            send(jnp.logical_not(root) & down, own(k), relay.at[z, k], s_recv.at[z, k], p, a - 2)
        for d in range(1, npix):
            send(here, own(k), l_ref(p, k), l_recv.at[p, k], mixed(p, d, npix), a)
    for k in range(chunks):
        to_twin(root, own(k), p, k)

    own_rows = pl.ds(pl.multiple_of(p * rows, rows), rows)
    keep_l = pltpu.make_async_copy(mj, lhs.at[own_rows, :], local_sem.at[0])
    keep_l.start()

    def term_step(i, acc):
        at = pl.ds(pl.multiple_of(i * 128, 128), 128)
        tile = mj[:, at].astype(F32)
        terms_f[p, :, at] = jnp.sum(tile * col[:, 1:2], axis=0, keepdims=True)
        return acc + tile * row[1:2, at]

    acc = lax.fori_loop(0, cols // 128, term_step, jnp.zeros((rows, 128), F32))
    terms_s[a] = jnp.sum(acc.T, axis=0, keepdims=True)
    for d in range(1, npix):
        send(here, terms_f.at[p], terms_f.at[p], f_recv.at[p], mixed(p, d, npix), a)
    for d in range(1, nact):
        send(here, terms_s.at[a], terms_s.at[a], p_recv.at[a], p, lax.rem(a + d, nact))

    events = []

    def on_l(d, k):
        def run():
            q = mixed(p, d, npix)
            arrived(l_ref(q, k), l_recv.at[q, k])
            if k >= via_line:
                along_line(root, l_ref(q, k), q, k)
            to_twin(root, l_ref(q, k), q, k)

        return run

    def on_s(dist, sign, k):
        def run():
            g = z - sign * dist
            there = (g >= 0) & (g < ngrp) & (g != p)
            slot = jnp.clip(g, 0, ngrp - 1)

            @pl.when(there)
            def _():
                arrived(relay.at[slot, k], s_recv.at[slot, k])

            if sign > 0:
                send(there & up, relay.at[slot, k], relay.at[slot, k], s_recv.at[slot, k], p, a + 2)
            else:
                send(there & down, relay.at[slot, k], relay.at[slot, k], s_recv.at[slot, k], p, a - 2)
            send(there, relay.at[slot, k], r_ref(p, k), r_recv.at[p, k], slot, a)

        return run

    def on_r(d, k):
        def run():
            q = mixed(p, d, npix)
            other = jnp.logical_not(root)

            @pl.when(other)
            def _():
                arrived(r_ref(q, k), r_recv.at[q, k])

            if d == 0 or k >= via_line:
                along_line(other, r_ref(q, k), q, k)
            to_twin(other, r_ref(q, k), q, k)

        return run

    unit = 4.0 / chunks
    for k in range(chunks):
        for d in range(1, npix):
            events.append((12 * unit * (k + 1) + 0.01 * d, on_l(d, k)))
        if k < via_line:
            for dist in range(1, ngrp):
                for sign in (1, -1):
                    events.append((6 * unit * (k + 1) + 18 * (dist - 1), on_s(dist, sign, k)))
        for d in range(npix):
            if d == 0:
                when = 6 * unit * (k + 1) + 12
            elif k >= via_line:
                when = 12 * unit * (k + 1) + 18
            else:
                when = 100 + k
            events.append((when, on_r(d, k)))
    events.sort(key=lambda e: e[0])
    for _, run in events:
        run()

    keep_l.wait()

    @pl.when(root)
    def _():
        copy = pltpu.make_async_copy(lhs, rhs.at[:, my_half], local_sem.at[1])
        copy.start()
        copy.wait()

    for d in range(1, npix):
        q = mixed(p, d, npix)
        arrived(terms_f.at[q], f_recv.at[q])
    proj[...] = functools.reduce(lambda x, y: x + y, [terms_f[q] for q in range(npix)])
    for d in range(1, nact):
        b = lax.rem(a + d, nact)
        arrived(terms_s.at[b], p_recv.at[b])
    pred[...] = functools.reduce(lambda x, y: x + y, [terms_s[b] for b in range(nact)])
    for q in range(npix):
        for k in range(chunks):
            ref = rhs.at[at_rows(q, k), other_half]
            arrived(ref, t_recv.at[q, k])
    for cond, make in pending:

        @pl.when(cond)
        def _():
            make().wait_send()


def gathered(npix, nact, jacobian, dark_field, update, pixel_mask, act_mask):
    rows, cols = jacobian.shape
    chunks, via_line = 4, 3
    ngrp = nact // 2
    pm = pixel_mask.astype(F32)
    am = act_mask.astype(F32)
    col = jnp.stack([pm, pm * dark_field], axis=1)
    row = jnp.stack([am, am * update], axis=0)
    n_sends = 0
    n_sends += chunks * (2 + npix - 1 + 1) + 2 * via_line
    n_sends += npix - 1 + nact - 1
    n_sends += chunks * (npix - 1) + 2 * (chunks - via_line) * (npix - 1)
    n_sends += via_line * (ngrp - 1) * 2 * 2
    n_sends += chunks * npix + 2 * (chunks + (chunks - via_line) * (npix - 1))
    vmem = pl.BlockSpec(memory_space=pltpu.VMEM)
    hbm = pl.BlockSpec(memory_space=pl.ANY)
    dma = pltpu.SemaphoreType.DMA
    return pl.pallas_call(
        functools.partial(gather_kernel, npix, ngrp, chunks, via_line),
        out_shape=(
            jax.ShapeDtypeStruct((npix * rows, cols), BF16),
            jax.ShapeDtypeStruct((npix * rows, 2 * cols), BF16),
            jax.ShapeDtypeStruct((1, cols), F32),
            jax.ShapeDtypeStruct((1, rows), F32),
        ),
        in_specs=[vmem] * 3,
        out_specs=(hbm, hbm, vmem, vmem),
        scratch_shapes=[
            pltpu.VMEM((rows, cols), BF16),
            pltpu.VMEM((ngrp, via_line, rows // chunks, cols), BF16),
            pltpu.VMEM((npix, 1, cols), F32),
            pltpu.VMEM((nact, 1, rows), F32),
            dma((npix, chunks)),
            dma((npix, chunks)),
            dma((npix, chunks)),
            dma((ngrp, via_line)),
            dma((npix,)),
            dma((nact,)),
            dma((n_sends,)),
            dma((2,)),
        ],
        compiler_params=pltpu.CompilerParams(
            collective_id=0, has_side_effects=True, vmem_limit_bytes=40 * 1024 * 1024
        ),
    )(jacobian, col, row)


def local(npix, nact, jacobian, dark_field, update, pixel_mask, act_mask):
    lhs, rhs, projected, predicted = gathered(
        npix, nact, jacobian, dark_field, update, pixel_mask, act_mask
    )
    gram_matrix = lax.dot_general(lhs, rhs, (((0,), (0,)), ((), ())), preferred_element_type=F32)
    return gram_matrix, projected[0], predicted[0]


def solution(mesh):
    npix, nact = mesh.shape["pix"], mesh.shape["act"]
    return jax.shard_map(
        functools.partial(local, npix, nact),
        mesh=mesh,
        in_specs=(P("pix", "act"), P("pix"), P("act"), P("pix"), P("act")),
        out_specs=(P("act", "pix"), P("act"), P("pix")),
        check_vma=False,
    )
```

time: 315 us -> 139 us (0.44); the launches traced: 310 us -> 139 us
  blocking collectives: 146 us -> 0 us
  Pallas kernels: 0 us -> 102 us
  waiting for transfers between devices: 93.1 us -> 0 us
  between operations: 15.6 us -> 0.67 us
  local copies, waits for them, and re-layouts: 14.3 us -> 1.98 us
  starting transfers between devices: 6.18 us -> 0 us
    psum x2 -> x0, blocking collectives: 146 us -> none  [the longest x1 132 us: local(): projected = lax.psum(field_term, 'pix')]
    pallas_call x0 -> x1, Pallas kernels: none -> 102 us  [gathered(): pl.pallas_call(functools.partial(gather_kernel, npix, ngrp, chunks, via_l...]
    all_gather x2 -> x0, waiting for transfers between devices: 92.5 us -> none  [the longest x1 92.5 us: local(): full_rows = lax.all_gather(masked_jac, 'act', axis=1, tiled=True)]
    all_to_all x1 -> x0, local copies, waits for them, and re-layouts: 12.7 us -> none  [local(): lax.all_to_all(full_rows, 'pix', split_axis=1, concat_axis=0, tiled=True)]
    all_to_all x1 -> x0, starting transfers between devices: 6.13 us -> none  [local(): lax.all_to_all(full_rows, 'pix', split_axis=1, concat_axis=0, tiled=True)]
    dot_general x3 -> x1, matrix products: 32.8 us -> 29.9 us  [local(): lax.dot_general(lhs, rhs, (((0,), (0,)), ((), ())), preferred_element_typ...]
  transfers between devices with their start and end apart: 3 -> 0, of which waited for: 1 -> 0; matrix products, arithmetic and copies ran while one was open for 5% -> 0% of each run, Pallas kernels for 0% -> 0%
where the time goes in v1:
time: 139 us
  Pallas kernels  102 us (73%)
  matrix products  29.9 us (22%)
  other arithmetic  3.49 us (3%)
  local copies, waits for them, and re-layouts  1.98 us (1%)
    pallas_call x1, Pallas kernels, gathered(): pl.pallas_call(functools.partial(gather_kernel, npix, ngrp, chunks, via_l...  102 us
    dot_general x1, matrix products, local(): lax.dot_general(lhs, rhs, (((0,), (0,)), ((), ())), preferred_element_typ...  29.9 us

profile of v1, /device:TPU:5, one launch (start us, length us, event | category | flops | bytes accessed | tf_op | source)
XLA Modules:
  0.0 138.5 jit_solution(6824694670181846564)
XLA Ops:
  0.6 0.7 convert_element_type.6
  1.3 0.7 convert_multiply_fusion.1
  2.0 0.1 copy.10.col
  2.2 0.7 convert_element_type.7
  2.9 0.7 convert_multiply_fusion
  3.7 0.0 copy-start
  3.7 1.3 copy-done
  4.9 102.5 %shard_map.76 = (bf16[1024,2304]{1,0:T(8,128)(2,1)S(1)}, bf16[1024,4608]{1,0:T(8,128)(2,1)}, f32[1,2304]{1,0:T(1,128)S(1)}, f32[1,256]{1,0:T(1,128)S(1)}) custom-call(bf16[256,2304]{1,0:T(8,128)(2,1)S(1)} %copy-done, f32[256,2]{1,0:T(8,128)S(1)} %copy.10.col, f32[2,2304]{1,0:T(2,128)S(1)} %pad_maximum_fusion.row), custom_call_target="tpu_custom_call" | custom-call | tf_op jit(solution)/shard_map/pallas_call | solution.py:234
  107.4 29.9 %fusion = f32[2304,4608]{1,0:T(8,128)} fusion(bf16[1024,2304]{1,0:T(8,128)(2,1)S(1)} %get-tuple-element.7, bf16[1024,4608]{1,0:T(8,128)(2,1)} %get-tuple-element.8), kind=kOutput, calls=%fused_computation.4 | convolution fusion | flops 21743271936 | bytes 56623104 | tf_op jit(solution)/shard_map/dot_general | solution.py:268
  137.3 0.6 reduce
  138.0 0.6 copy.12
  (4 shorter events, 0.1 us)
Async XLA Ops:
  3.7 1.3 copy-start

commit v2 on v1

--- a/solution.py
+++ b/solution.py
@@ -10,6 +10,9 @@
 MESH = pl.DeviceIdType.MESH
 F32 = jnp.float32
 BF16 = jnp.bfloat16
+MIB = 1024 * 1024
+FIRST = 18
+SECOND = 9
 
 
 def mixed(index, step, size):
@@ -22,11 +25,12 @@
 
 
 def gather_kernel(
-    npix, ngrp, chunks, via_line, jac, col, row, lhs, rhs, proj, pred,
-    mj, relay, terms_f, terms_s, l_recv, r_recv, t_recv, s_recv, f_recv, p_recv, sends, local_sem,
+    npix, ngrp, chunks, via_line, early, jac, pmask, field, amask, update, lt, late, gram, proj, pred,
+    lhs, first, relay, terms_f, terms_s, l_recv, r_recv, t_recv, s_recv, f_recv, p_recv, sends, local_sem,
 ):
     rows, cols = jac.shape
-    ch = rows // chunks
+    wide = cols // chunks
+    lanes = wide // 128
     p = lax.axis_index("pix")
     a = lax.axis_index("act")
     z = a // 2
@@ -41,13 +45,25 @@
     for d in range(1, nact):
         pl.semaphore_signal(barrier, inc=1, device_id={"pix": p, "act": lax.rem(a + d, nact)}, device_id_type=MESH)
 
-    def mask_step(i, carry):
-        at = pl.ds(pl.multiple_of(i * 128, 128), 128)
-        keep = col[:, 0:1] * row[0:1, at] > 0
-        mj[:, at] = jnp.where(keep, jac[:, at].astype(F32), 0.0).astype(BF16)
+    def rows_of(q):
+        return pl.ds(pl.multiple_of(q * rows, rows), rows)
+
+    def down_rows(v):
+        return jnp.broadcast_to(v, (128, rows)).T
+
+    pm = pmask[...].astype(F32)
+    kept = down_rows(pm)
+    weighted = down_rows(pm * field[...])
+
+    def mask_step(k, carry):
+        for i in range(lanes):
+            at = pl.ds(pl.multiple_of((k * lanes + i) * 128, 128), 128)
+            keep = kept * amask[:, at].astype(F32) > 0
+            masked = jnp.where(keep, jac[:, at].astype(F32), 0.0)
+            lhs[k, rows_of(p), i * 128:(i + 1) * 128] = masked.astype(BF16)
         return carry
 
-    lax.fori_loop(0, cols // 128, mask_step, 0)
+    lax.fori_loop(0, chunks, mask_step, 0)
     pl.semaphore_wait(barrier, npix - 1 + nact - 1)
 
     pending = []
@@ -70,20 +86,23 @@
     def arrived(ref, sem):
         pltpu.make_async_copy(ref, ref, sem).wait()
 
-    def at_rows(q, k):
-        return pl.ds(pl.multiple_of(q * rows + k * ch, ch), ch)
-
-    my_half = pl.ds(pl.multiple_of(c * cols, 128), cols)
-    other_half = pl.ds(pl.multiple_of((1 - c) * cols, 128), cols)
+    my_half = pl.ds(pl.multiple_of(c * wide, 128), wide)
+    other_half = pl.ds(pl.multiple_of((1 - c) * wide, 128), wide)
+
+    def rhs(k):
+        return first.at[k] if k < early else late.at[k - early]
 
     def l_ref(q, k):
-        return lhs.at[at_rows(q, k), :]
+        return lhs.at[k, rows_of(q), :]
 
     def r_ref(q, k):
-        return rhs.at[at_rows(q, k), my_half]
+        return rhs(k).at[rows_of(q), my_half]
 
     def own(k):
-        return mj.at[pl.ds(k * ch, ch), :]
+        return l_ref(p, k)
+
+    def turn(q, k):
+        lt[k, :, pl.ds(pl.multiple_of(q * rows, rows), rows)] = lhs[k, rows_of(q), :].T
 
     up = z + 1 < ngrp
     down = z > 0
@@ -105,23 +124,24 @@
     for k in range(chunks):
         to_twin(root, own(k), p, k)
 
-    own_rows = pl.ds(pl.multiple_of(p * rows, rows), rows)
-    keep_l = pltpu.make_async_copy(mj, lhs.at[own_rows, :], local_sem.at[0])
-    keep_l.start()
-
-    def term_step(i, acc):
-        at = pl.ds(pl.multiple_of(i * 128, 128), 128)
-        tile = mj[:, at].astype(F32)
-        terms_f[p, :, at] = jnp.sum(tile * col[:, 1:2], axis=0, keepdims=True)
-        return acc + tile * row[1:2, at]
-
-    acc = lax.fori_loop(0, cols // 128, term_step, jnp.zeros((rows, 128), F32))
+    def term_step(k, acc):
+        for i in range(lanes):
+            at = pl.ds(pl.multiple_of((k * lanes + i) * 128, 128), 128)
+            tile = lhs[k, rows_of(p), i * 128:(i + 1) * 128].astype(F32)
+            terms_f[p, :, at] = jnp.sum(tile * weighted, axis=0, keepdims=True)
+            acc = acc + tile * (amask[:, at].astype(F32) * update[:, at])
+        return acc
+
+    acc = lax.fori_loop(0, chunks, term_step, jnp.zeros((rows, 128), F32))
     terms_s[a] = jnp.sum(acc.T, axis=0, keepdims=True)
     for d in range(1, npix):
         send(here, terms_f.at[p], terms_f.at[p], f_recv.at[p], mixed(p, d, npix), a)
     for d in range(1, nact):
         send(here, terms_s.at[a], terms_s.at[a], p_recv.at[a], p, lax.rem(a + d, nact))
 
+    for k in range(chunks):
+        turn(p, k)
+
     events = []
 
     def on_l(d, k):
@@ -131,6 +151,7 @@
             if k >= via_line:
                 along_line(root, l_ref(q, k), q, k)
             to_twin(root, l_ref(q, k), q, k)
+            turn(q, k)
 
         return run
 
@@ -164,6 +185,35 @@
             if d == 0 or k >= via_line:
                 along_line(other, r_ref(q, k), q, k)
             to_twin(other, r_ref(q, k), q, k)
+
+        return run
+
+    def on_root():
+        @pl.when(root)
+        def _():
+            copies = [
+                pltpu.make_async_copy(lhs.at[k], rhs(k).at[:, my_half], local_sem.at[k])
+                for k in range(chunks)
+            ]
+            for copy in copies:
+                copy.start()
+            for copy in copies:
+                copy.wait()
+
+    def on_twin(k):
+        def run():
+            for q in range(npix):
+                arrived(rhs(k).at[rows_of(q), other_half], t_recv.at[q, k])
+
+        return run
+
+    def on_product(k):
+        def run():
+            def step(j, carry):
+                gram[k, j] = jnp.dot(lt[j], first[k], preferred_element_type=F32)
+                return carry
+
+            lax.fori_loop(0, chunks, step, 0)
 
         return run
 
@@ -183,17 +233,15 @@
             else:
                 when = 100 + k
             events.append((when, on_r(d, k)))
+        if k < early:
+            events.append((100.4 + k, on_twin(k)))
+            events.append((100.5 + k, on_product(k)))
+        else:
+            events.append((200 + k, on_twin(k)))
+    events.append((99, on_root))
     events.sort(key=lambda e: e[0])
     for _, run in events:
         run()
-
-    keep_l.wait()
-
-    @pl.when(root)
-    def _():
-        copy = pltpu.make_async_copy(lhs, rhs.at[:, my_half], local_sem.at[1])
-        copy.start()
-        copy.wait()
 
     for d in range(1, npix):
         q = mixed(p, d, npix)
@@ -203,10 +251,6 @@
         b = lax.rem(a + d, nact)
         arrived(terms_s.at[b], p_recv.at[b])
     pred[...] = functools.reduce(lambda x, y: x + y, [terms_s[b] for b in range(nact)])
-    for q in range(npix):
-        for k in range(chunks):
-            ref = rhs.at[at_rows(q, k), other_half]
-            arrived(ref, t_recv.at[q, k])
     for cond, make in pending:
 
         @pl.when(cond)
@@ -214,14 +258,49 @@
             make().wait_send()
 
 
-def gathered(npix, nact, jacobian, dark_field, update, pixel_mask, act_mask):
+def rest_kernel(early, lt, rhs, done, gram, product, sems):
+    chunks, wide, _ = lt.shape
+    cols = chunks * wide
+    copies = []
+    for k in range(early):
+        for h in range(2):
+            for j in range(chunks):
+                copy = pltpu.make_async_copy(
+                    done.at[k, j, :, h * wide:(h + 1) * wide],
+                    gram.at[j * wide:(j + 1) * wide, h * cols + k * wide:h * cols + (k + 1) * wide],
+                    sems.at[k, h, j],
+                )
+                copy.start()
+                copies.append(copy)
+    held = []
+    for k in range(early, chunks):
+        for j in range(chunks):
+            slot = len(held) % product.shape[0]
+            if len(held) >= product.shape[0]:
+                for copy in held[len(held) - product.shape[0]]:
+                    copy.wait()
+            product[slot] = jnp.dot(lt[j], rhs[k - early], preferred_element_type=F32)
+            held.append([])
+            for h in range(2):
+                copy = pltpu.make_async_copy(
+                    product.at[slot, :, h * wide:(h + 1) * wide],
+                    gram.at[j * wide:(j + 1) * wide, h * cols + k * wide:h * cols + (k + 1) * wide],
+                    sems.at[k, h, j],
+                )
+                copy.start()
+                held[-1].append(copy)
+    for pair in held[-product.shape[0]:]:
+        copies += pair
+    for copy in copies:
+        copy.wait()
+
+
+def local(npix, nact, jacobian, dark_field, update, pixel_mask, act_mask):
     rows, cols = jacobian.shape
-    chunks, via_line = 4, 3
+    chunks = next(n for n in (6, 3, 2, 1) if cols % (128 * n) == 0)
+    via_line, early = max(1, chunks * 5 // 6), chunks * 2 // 3
+    wide = cols // chunks
     ngrp = nact // 2
-    pm = pixel_mask.astype(F32)
-    am = act_mask.astype(F32)
-    col = jnp.stack([pm, pm * dark_field], axis=1)
-    row = jnp.stack([am, am * update], axis=0)
     n_sends = 0
     n_sends += chunks * (2 + npix - 1 + 1) + 2 * via_line
     n_sends += npix - 1 + nact - 1
@@ -231,19 +310,21 @@
     vmem = pl.BlockSpec(memory_space=pltpu.VMEM)
     hbm = pl.BlockSpec(memory_space=pl.ANY)
     dma = pltpu.SemaphoreType.DMA
-    return pl.pallas_call(
-        functools.partial(gather_kernel, npix, ngrp, chunks, via_line),
+    lt, rhs, done, projected, predicted = pl.pallas_call(
+        functools.partial(gather_kernel, npix, ngrp, chunks, via_line, early),
         out_shape=(
-            jax.ShapeDtypeStruct((npix * rows, cols), BF16),
-            jax.ShapeDtypeStruct((npix * rows, 2 * cols), BF16),
+            jax.ShapeDtypeStruct((chunks, wide, npix * rows), BF16),
+            jax.ShapeDtypeStruct((chunks - early, npix * rows, 2 * wide), BF16),
+            jax.ShapeDtypeStruct((early, chunks, wide, 2 * wide), F32),
             jax.ShapeDtypeStruct((1, cols), F32),
             jax.ShapeDtypeStruct((1, rows), F32),
         ),
-        in_specs=[vmem] * 3,
-        out_specs=(hbm, hbm, vmem, vmem),
+        in_specs=[vmem] * 5,
+        out_specs=(vmem,) * 5,
         scratch_shapes=[
-            pltpu.VMEM((rows, cols), BF16),
-            pltpu.VMEM((ngrp, via_line, rows // chunks, cols), BF16),
+            pltpu.VMEM((chunks, npix * rows, wide), BF16),
+            pltpu.VMEM((early, npix * rows, 2 * wide), BF16),
+            pltpu.VMEM((ngrp, via_line, rows, wide), BF16),
             pltpu.VMEM((npix, 1, cols), F32),
             pltpu.VMEM((nact, 1, rows), F32),
             dma((npix, chunks)),
@@ -253,19 +334,23 @@
             dma((npix,)),
             dma((nact,)),
             dma((n_sends,)),
-            dma((2,)),
+            dma((chunks,)),
         ],
         compiler_params=pltpu.CompilerParams(
-            collective_id=0, has_side_effects=True, vmem_limit_bytes=40 * 1024 * 1024
+            collective_id=0, has_side_effects=True, vmem_limit_bytes=FIRST * MIB
         ),
-    )(jacobian, col, row)
-
-
-def local(npix, nact, jacobian, dark_field, update, pixel_mask, act_mask):
-    lhs, rhs, projected, predicted = gathered(
-        npix, nact, jacobian, dark_field, update, pixel_mask, act_mask
-    )
-    gram_matrix = lax.dot_general(lhs, rhs, (((0,), (0,)), ((), ())), preferred_element_type=F32)
+    )(jacobian, pixel_mask[None], dark_field[None], act_mask[None], update[None])
+    gram_matrix = pl.pallas_call(
+        functools.partial(rest_kernel, early),
+        out_shape=jax.ShapeDtypeStruct((cols, 2 * cols), F32),
+        in_specs=[vmem, vmem, hbm],
+        out_specs=hbm,
+        scratch_shapes=[
+            pltpu.VMEM((4, wide, 2 * wide), F32),
+            dma((chunks, 2, chunks)),
+        ],
+        compiler_params=pltpu.CompilerParams(vmem_limit_bytes=SECOND * MIB),
+    )(lt, rhs, done)
     return gram_matrix, projected[0], predicted[0]
 
 

time: 139 us -> 143 us (1.029)
  Pallas kernels: 102 us -> 137 us
  matrix products: 29.9 us -> 0 us
  other arithmetic: 3.49 us -> 0.63 us
  local copies, waits for them, and re-layouts: 1.98 us -> 4.61 us
    pallas_call x1 -> x2, Pallas kernels: 102 us -> 137 us  [the longest x1 118 us: local(): pl.pallas_call(functools.partial(gather_kernel, npix, ngrp, chunks, via_l...]
    dot_general x1 -> x0, matrix products: 29.9 us -> none  [local(): lax.dot_general(lhs, rhs, (((0,), (0,)), ((), ())), preferred_element_typ...]
    unnamed x3 -> x7, local copies, waits for them, and re-layouts: 1.83 us -> 3.19 us
where the time goes in v2:
time: 143 us; the launch traced here: 142 us
  Pallas kernels  137 us (96%)
  local copies, waits for them, and re-layouts  4.61 us (3%)
    pallas_call x1, Pallas kernels, local(): pl.pallas_call(functools.partial(gather_kernel, npix, ngrp, chunks, via_l...  118 us
    pallas_call x1, Pallas kernels, local(): pl.pallas_call(functools.partial(rest_kernel, early), out_shape=jax.Shape...  19.1 us
    unnamed x7, local copies, waits for them, and re-layouts  3.19 us

profile of v2, /device:TPU:5, one launch (start us, length us, event | category | flops | bytes accessed | tf_op | source)
XLA Modules:
  0.0 142.5 jit_solution(13324533563564940193)
XLA Ops:
  0.6 0.7 broadcast_in_dim.14.amask
  1.3 0.7 broadcast_in_dim.15.update
  2.1 0.0 copy-start
  2.1 1.3 copy-done
  3.3 0.0 copy-start.1
  3.3 0.7 copy-done.1
  4.0 0.0 copy-start.2
  4.0 0.7 copy-done.2
  4.7 117.5 %shard_map.76 = (bf16[6,384,1024]{2,1,0:T(8,128)(2,1)S(1)}, bf16[2,1024,768]{2,1,0:T(8,128)(2,1)S(1)}, f32[4,6,384,768]{3,2,1,0:T(8,128)S(1)}, f32[1,2304]{1,0:T(1,128)S(1)}, f32[1,256]{1,0:T(1,128)S(1)}) custom-call(bf16[256,2304]{1,0:T(8,128)(2,1)S(1)} %copy-done, s32[1,256]{1,0:T(1,128)S(1)} %bitcast.3, f32[1,256]{1,0:T(1,128)S(1)} %bitcast.4, ...), custom_call_target="tpu_custom_call" | custom-call | tf_op jit(solution)/shard_map/pallas_call | solution.py:313
  122.2 19.1 %shard_map.77 = f32[2304,4608]{1,0:T(8,128)} custom-call(bf16[6,384,1024]{2,1,0:T(8,128)(2,1)S(1)} %get-tuple-element.8.lt, bf16[2,1024,768]{2,1,0:T(8,128)(2,1)S(1)} %get-tuple-element.9.rhs, f32[4,6,384,768]{3,2,1,0:T(8,128)S(1)} %get-tuple-element.10.done), custom_call_target="tpu_custom_call" | custom-call | tf_op jit(solution)/shard_map/pallas_call | solution.py:343
  141.3 0.6 reduce
  141.9 0.6 copy.9
Async XLA Ops:
  2.1 1.3 copy-start
  3.3 0.7 copy-start.1
  4.0 0.7 copy-start.2

commit v3 on v2

--- a/solution.py
+++ b/solution.py
@@ -207,13 +207,9 @@
 
         return run
 
-    def on_product(k):
-        def run():
-            def step(j, carry):
-                gram[k, j] = jnp.dot(lt[j], first[k], preferred_element_type=F32)
-                return carry
-
-            lax.fori_loop(0, chunks, step, 0)
+    def on_product(k, j):
+        def run():
+            gram[k, j] = jnp.dot(lt[j], first[k], preferred_element_type=F32)
 
         return run
 
@@ -231,14 +227,15 @@
             elif k >= via_line:
                 when = 12 * unit * (k + 1) + 18
             else:
-                when = 100 + k
+                when = 67 + 4 * unit * k
             events.append((when, on_r(d, k)))
         if k < early:
-            events.append((100.4 + k, on_twin(k)))
-            events.append((100.5 + k, on_product(k)))
+            events.append((69 + 4 * unit * k, on_twin(k)))
+            for j in range(chunks):
+                events.append((69.5 + 4 * unit * k + j * 0.5, on_product(k, j)))
         else:
             events.append((200 + k, on_twin(k)))
-    events.append((99, on_root))
+    events.append((49, on_root))
     events.sort(key=lambda e: e[0])
     for _, run in events:
         run()
@@ -298,7 +295,7 @@
 def local(npix, nact, jacobian, dark_field, update, pixel_mask, act_mask):
     rows, cols = jacobian.shape
     chunks = next(n for n in (6, 3, 2, 1) if cols % (128 * n) == 0)
-    via_line, early = max(1, chunks * 5 // 6), chunks * 2 // 3
+    via_line, early = max(1, chunks * 5 // 6), max(1, chunks // 3)
     wide = cols // chunks
     ngrp = nact // 2
     n_sends = 0

time: 143 us -> 139 us (0.972)
  the two profiles are of different devices: /device:TPU:5 before, /device:TPU:25 now
where the time goes in v3:
time: 139 us
  Pallas kernels  133 us (96%)
  local copies, waits for them, and re-layouts  4.61 us (3%)
    pallas_call x1, Pallas kernels, local(): pl.pallas_call(functools.partial(gather_kernel, npix, ngrp, chunks, via_l...  106 us
    pallas_call x1, Pallas kernels, local(): pl.pallas_call(functools.partial(rest_kernel, early), out_shape=jax.Shape...  26.7 us
    unnamed x7, local copies, waits for them, and re-layouts  3.19 us

profile of v3, /device:TPU:25, one launch (start us, length us, event | category | flops | bytes accessed | tf_op | source)
XLA Modules:
  0.0 138.8 jit_solution(16381405436184457675)
XLA Ops:
  0.6 0.7 broadcast_in_dim.14.amask
  1.3 0.7 broadcast_in_dim.15.update
  2.1 0.0 copy-start
  2.1 1.3 copy-done
  3.3 0.0 copy-start.1
  3.3 0.7 copy-done.1
  4.0 0.0 copy-start.2
  4.0 0.7 copy-done.2
  4.7 106.2 %shard_map.76 = (bf16[6,384,1024]{2,1,0:T(8,128)(2,1)S(1)}, bf16[4,1024,768]{2,1,0:T(8,128)(2,1)S(1)}, f32[2,6,384,768]{3,2,1,0:T(8,128)S(1)}, f32[1,2304]{1,0:T(1,128)S(1)}, f32[1,256]{1,0:T(1,128)S(1)}) custom-call(bf16[256,2304]{1,0:T(8,128)(2,1)S(1)} %copy-done, s32[1,256]{1,0:T(1,128)S(1)} %bitcast.3, f32[1,256]{1,0:T(1,128)S(1)} %bitcast.4, ...), custom_call_target="tpu_custom_call" | custom-call | tf_op jit(solution)/shard_map/pallas_call | solution.py:310
  110.9 26.7 %shard_map.77 = f32[2304,4608]{1,0:T(8,128)} custom-call(bf16[6,384,1024]{2,1,0:T(8,128)(2,1)S(1)} %get-tuple-element.8.lt, bf16[4,1024,768]{2,1,0:T(8,128)(2,1)S(1)} %get-tuple-element.9.rhs, f32[2,6,384,768]{3,2,1,0:T(8,128)S(1)} %get-tuple-element.10.done), custom_call_target="tpu_custom_call" | custom-call | tf_op jit(solution)/shard_map/pallas_call | solution.py:340
  137.6 0.6 reduce
  138.2 0.6 copy.9
Async XLA Ops:
  2.1 1.3 copy-start
  3.3 0.7 copy-start.1
  4.0 0.7 copy-start.2
